TPU v7x, 32 devices: a whole 2x2x4 slice. The times are simulated.
32 devices in a mesh: rows: 16 (over z, y, x), tm: 2 (over core).
Axes of the slice: x: 2, y: 2, z: 4, core: 2. Of those that a mesh axis runs over, the one named last changes fastest.
Arguments:
- snapshots: bfloat16 [262144, 256], P('rows', 'tm'), may hold values from -6 to 6
- basis: bfloat16 [262144, 32], P(('rows', 'tm')), may hold values from -0.01171875 to 0.01171875
Outputs:
- gram: float32 [560, 560], replicated
- rhs: float32 [560, 32], replicated
All inputs are finite; a program needn't handle non-finite values.
Results may differ from a plain program's by a relative error of at most 0.0003.
Values may be sent and summed in bfloat16 or wider, within the bound.
A program may use at most 64 MiB of HBM per device.

v0:
```python
import jax
import jax.numpy as jnp
import numpy as np
from jax import lax
from jax.sharding import PartitionSpec as P


def from_behind(block, axis, distance):
    devices = range(lax.axis_size(axis))
    route = [(i - distance, i) for i in devices if i - distance in devices]
    return lax.ppermute(block, axis, route)


def build_sums(projected, velocity, first_step, total_steps):
    series = projected.T
    num_modes = series.shape[1]
    weight = (first_step + jnp.arange(series.shape[0]) < total_steps - 1).astype(jnp.float32)
    upper_pair = np.triu_indices(num_modes)
    quadratic = series[:, upper_pair[0]] * series[:, upper_pair[1]]
    features = jnp.concatenate([series, quadratic], axis=1)
    weighted = features * weight[:, None]
    gram_part = jnp.dot(weighted.T, features, precision=lax.Precision.HIGHEST)
    rhs_part = jnp.dot(weighted.T, velocity.T, precision=lax.Precision.HIGHEST)
    return (gram_part, rhs_part)


def shards(snapshots, basis):
    rows_count, step_count = snapshots.shape
    partial_value = jnp.einsum(
        "nr,nt->rt",
        lax.all_gather(basis, "tm", axis=0, tiled=True),
        snapshots,
        preferred_element_type=jnp.float32,
    )
    first_next = from_behind(partial_value[:, :1], "tm", -1)
    velocity_part = jnp.concatenate([partial_value[:, 1:], first_next], axis=1) - partial_value
    group_size = lax.axis_size("rows")
    share = step_count // group_size
    total_steps = step_count * lax.axis_size("tm")
    first_step = lax.axis_index("tm") * step_count + lax.axis_index("rows") * share
    whole_proj, whole_vel = lax.psum((partial_value, velocity_part), "rows")
    column = lax.axis_index("rows") * share
    projected = lax.dynamic_slice_in_dim(whole_proj, column, share, 1)
    velocity = lax.dynamic_slice_in_dim(whole_vel, column, share, 1)
    gram_part, rhs_part = build_sums(projected, velocity, first_step, total_steps)
    gram_sum, rhs_sum = lax.psum((gram_part, rhs_part), ("rows", "tm"))
    return (gram_sum / total_steps, rhs_sum / total_steps)


def solution(mesh):
    in_specs = (P("rows", "tm"), P(("rows", "tm"), None))
    out_specs = (P(), P())
    return jax.shard_map(shards, mesh=mesh, in_specs=in_specs, out_specs=out_specs, check_vma=False)
```

profile of v0, /device:TPU:0, one launch (start us, length us, event | category | flops | bytes accessed | tf_op | source)
XLA Modules:
  0.0 249.2 jit_solution(8498607268534217137)
XLA Ops:
  7.2 0.0 all-gather.2.cloned.1.call-start
  7.2 0.7 all-gather.2.cloned.1.call-update
  7.9 0.0 all-reduce.4.cloned.1.call-start
  8.0 0.7 pad_clamp_fusion.1
  8.7 0.7 pad_clamp_fusion
  9.4 12.0 %all-gather.2.cloned.1.call-done = bf16[16384,32]{0,1:T(8,128)(2,1)} async-done(((bf16[8192,32]{0,1:T(8,128)(2,1)}), bf16[16384,32]{0,1:T(8,128)(2,1)}) %all-gather.2.cloned.1.call-update) | async-done | bytes 1048592 | tf_op jit(solution)/shard_map/all_gather | solution.py:31
  21.3 3.3 %fusion.10 = f32[32,128]{1,0:T(8,128)S(1)} fusion(bf16[16384,32]{0,1:T(8,128)(2,1)} %all-gather.2.cloned.1.call-done, bf16[16384,128]{1,0:T(8,128)(2,1)} %param.6), kind=kOutput, calls=%fused_computation.21 | convolution fusion | flops 134217728 | bytes 5259264 | tf_op jit(solution)/shard_map/nr,nt->rt/dot_general | solution.py:29
  24.6 1.3 collective-permute-start
  25.9 0.1 slice.12
  25.9 1.7 collective-permute-done
  27.7 0.1 maximum_subtract_fusion
  27.7 77.0 %all-reduce.1 = (f32[32,128]{1,0:T(8,128)S(1)}, f32[32,128]{1,0:T(8,128)S(1)}) all-reduce(f32[32,128]{1,0:T(8,128)S(1)} %fusion.10, f32[32,128]{1,0:T(8,128)S(1)} %maximum_subtract_fusion), channel_id=1, replica_groups=mesh['rows'=16,'tm'=2] {'rows'}, use_global_device_ids=true, to_apply=%region_0.0 | all-reduce | flops 8192 | bytes 65536 | tf_op jit(solution)/shard_map/psum | solution.py:41
  104.7 0.1 dynamic-slice_bitcast_fusion
  104.8 0.1 copy.8
  104.9 1.6 gather_fusion.1
  106.5 1.6 gather_fusion
  108.1 0.1 copy.9
  108.2 2.6 %fusion.2 = f32[560,560]{1,0:T(8,128)} fusion(f32[8,528]{1,0:T(8,128)S(1)} %copy.9, f32[8,32]{1,0:T(8,128)S(1)} %copy.8, f32[8]{0:T(128)S(1)} %compare_convert_fusion), kind=kOutput, calls=%fused_computation.7 | convolution fusion | flops 30119040 | bytes 1272352 | tf_op jit(solution)/shard_map/dot_general | solution.py:22
  110.8 0.9 fusion
  111.7 0.0 all-reduce.4.cloned.1.call-update
  111.7 127.4 %all-reduce.4.cloned.1.call-done = (f32[560,560]{1,0:T(8,128)}, f32[560,32]{0,1:T(8,128)}) async-done(((f32[560,560]{1,0:T(8,128)}, f32[560,32]{0,1:T(8,128)}), (f32[560,560]{1,0:T(8,128)}, f32[560,32]{0,1:T(8,128)})) %all-reduce.4.cloned.1.call-update) | async-done | bytes 1326096 | tf_op jit(solution)/shard_map/psum | solution.py:46
  239.1 2.6 %broadcast_multiply_fusion = f32[560,560]{1,0:T(8,128)} fusion(f32[560,560]{1,0:T(8,128)} %get-tuple-element.2), kind=kLoop, calls=%fused_computation.2 | loop fusion | flops 313600 | bytes 2508800 | tf_op jit(solution)/shard_map/div | solution.py:47
  241.7 0.0 copy-done
  241.7 0.6 broadcast_multiply_fusion.1
  (3 shorter events, 0.0 us)
Async XLA Ops:
  7.2 14.1 %all-gather.2.cloned.1.call-start = ((), (), s32[]{:S(2)}) async-start(), calls=%async_computation | async-start | bytes 1572864 | tf_op jit(solution)/shard_map/all_gather | solution.py:31
  7.9 231.2 %all-reduce.4.cloned.1.call-start = ((), (), s32[]{:S(2)}) async-start(), calls=%async_computation.1 | async-start | bytes 3031040 | tf_op jit(solution)/shard_map/psum | solution.py:46
  24.6 3.1 %collective-permute-start = (f32[32,1]{1,0:T(8,128)S(1)}, f32[32,1]{1,0:T(8,128)S(1)}, u32[]{:S(2)}, u32[]{:S(2)}) collective-permute-start(f32[32,1]{1,0:T(8,128)S(1)} %bitcast.7), channel_id=1, source_target_pairs={{1,0},{3,2},{5,4},{7,6},{9,8},{11,10},{13,12},{15,14},{17,16},{19,... | collective-permute-start | bytes 392 | tf_op jit(solution)/shard_map/ppermute | solution.py:11
  239.1 2.6 %copy-start = (f32[560,32]{0,1:T(8,128)S(1)}, f32[560,32]{0,1:T(8,128)}, u32[]{:S(2)}) copy-start(f32[560,32]{0,1:T(8,128)} %get-tuple-element.3) | copy-start | bytes 215044
Sparse Core Ops, SparseCore 0:
  9.5 11.7 all-gather.1
  111.8 127.2 all-reduce.3
where the time goes:
time: 249 us
  waiting for transfers between devices  142 us (57%)
  blocking collectives  77 us (31%)
  between operations  14.1 us (6%)
  matrix products  6.72 us (3%)
  other arithmetic  4.73 us (2%)
  local copies, waits for them, and re-layouts  3.5 us (1%)
    psum x1, waiting for transfers between devices, shards(): gram_sum, rhs_sum = lax.psum((gram_part, rhs_part), ('rows', 'tm'))  127 us
    psum x1, blocking collectives, shards(): whole_proj, whole_vel = lax.psum((partial_value, velocity_part), 'rows')  77 us
    all_gather x1, waiting for transfers between devices, shards(): lax.all_gather(basis, 'tm', axis=0, tiled=True)  12 us
  transfers between devices with their start and end apart: 3, of which 3 were waited for; matrix products, arithmetic and copies ran while one was open for 1% of the time, Pallas kernels for 0%

commit v1 on v0

v1 whole, which is shorter than its diff:
```python
import functools

import jax
import jax.numpy as jnp
from jax import lax
from jax.experimental import pallas as pl
from jax.experimental.pallas import tpu as pltpu
from jax.sharding import PartitionSpec as P

MESH = pl.DeviceIdType.MESH
CHUNKS = 2


def project_kernel(groups, blocks, owners, snap_hbm, basis_hbm, out_ref, snap, basis, part, landed, gathered,
                   snap_sem, basis_sem, send_basis, recv_basis, send_part, recv_part, send_sum, recv_sum):
    row, block = lax.axis_index("rows"), lax.axis_index("tm")
    world = groups * blocks
    modes, depth = basis_hbm.shape
    share = modes // owners
    piece = depth // CHUNKS

    own_basis = pltpu.make_async_copy(basis_hbm, basis.at[block], basis_sem)
    own_basis.start()
    loads = []
    for i in range(blocks):
        at = lax.rem(block + i, blocks)
        for c in range(CHUNKS):
            span = pl.ds(pl.multiple_of(at * depth + c * piece, 256), piece)
            load = pltpu.make_async_copy(snap_hbm.at[span], snap.at[span], snap_sem.at[i * CHUNKS + c])
            load.start()
            loads.append((load, span))

    barrier = pltpu.get_barrier_semaphore()
    me = row * blocks + block

    def greet(d, carry):
        other = lax.rem(me + d, world)
        pl.semaphore_signal(barrier, inc=1, device_id=(other // blocks, lax.rem(other, blocks)), device_id_type=MESH)
        return carry

    lax.fori_loop(1, world, greet, 0)
    own_basis.wait()
    pl.semaphore_wait(barrier, world - 1)

    sends = []
    for d in range(1, blocks):
        send = pltpu.make_async_remote_copy(
            src_ref=basis.at[block], dst_ref=basis.at[block], send_sem=send_basis.at[d - 1], recv_sem=recv_basis.at[d - 1],
            device_id=(row, lax.rem(block + d, blocks)), device_id_type=MESH)
        send.start()
        sends.append(send)

    total = jnp.zeros((modes, snap.shape[1]), jnp.float32)
    for i in range(blocks):
        at = lax.rem(block + i, blocks)
        if i > 0:
            pltpu.make_async_copy(basis.at[at], basis.at[at], recv_basis.at[blocks - i - 1]).wait()
        for c in range(CHUNKS):
            load, span = loads[i * CHUNKS + c]
            load.wait()
            total += jnp.dot(basis[at, :, c * piece:(c + 1) * piece], snap[span, :], preferred_element_type=jnp.float32)
    for k in range(owners):
        part[k] = total[k * share:(k + 1) * share]

    def scatter(d, carry):
        owner = lax.rem(row + d, owners)

        @pl.when(owner != row)
        def _():
            slot = lax.rem(row - owner + groups, groups) - 1
            pltpu.make_async_remote_copy(
                src_ref=part.at[owner], dst_ref=landed.at[slot], send_sem=send_part, recv_sem=recv_part,
                device_id=(owner, block), device_id_type=MESH).start()

        return carry

    lax.fori_loop(0, owners, scatter, 0)

    def reduce_and_spread():
        pltpu.make_async_copy(landed, landed, recv_part).wait()
        mine = block * owners + row
        gathered[mine] = part[row] + jnp.sum(landed[...], axis=0)

        def spread(d, carry):
            other = lax.rem(me + d, world)
            pltpu.make_async_remote_copy(
                src_ref=gathered.at[mine], dst_ref=gathered.at[mine], send_sem=send_sum, recv_sem=recv_sum,
                device_id=(other // blocks, lax.rem(other, blocks)), device_id_type=MESH).start()
            return carry

        lax.fori_loop(1, world, spread, 0)
        rest = gathered.at[pl.ds(0, owners * blocks - 1)]
        pltpu.make_async_copy(rest, rest, recv_sum).wait()
        for _ in range(groups // owners - 1):
            pltpu.make_async_copy(gathered, gathered, send_sum).wait()
        pltpu.make_async_copy(rest, rest, send_sum).wait()
        sent = part.at[pl.ds(0, owners - 1)]
        pltpu.make_async_copy(sent, sent, send_part).wait()

    if owners == groups:
        reduce_and_spread()
    else:
        pl.when(row < owners)(reduce_and_spread)

        @pl.when(row >= owners)
        def _():
            pltpu.make_async_copy(gathered, gathered, recv_sum).wait()
            pltpu.make_async_copy(part, part, send_part).wait()

    for send in sends:
        send.wait_send()
    steps = snap.shape[1]
    for t in range(blocks):
        for k in range(owners):
            out_ref[k * share:(k + 1) * share, t * steps:(t + 1) * steps] = gathered[t * owners + k]


def gram_kernel(proj_ref, gram_ref, rhs_ref, features, high, low):
    modes, steps = proj_ref.shape
    projected = proj_ref[...]
    velocity = pltpu.roll(projected, steps - 1, 1) - projected
    series = jnp.where(lax.broadcasted_iota(jnp.int32, projected.shape, 1) < steps - 1, projected, 0.0)
    features[0:modes, :] = series
    at = modes
    for i in range(modes):
        features[at:at + modes - i, :] = series[i:i + 1, :] * series[i:, :]
        at += modes - i
    whole = features[...]
    top = whole.astype(jnp.bfloat16)
    high[...] = top
    low[...] = (whole - top.astype(jnp.float32)).astype(jnp.bfloat16)

    def times(a, b):
        return lax.dot_general(a, b, (((1,), (1,)), ((), ())), preferred_element_type=jnp.float32)

    scale = 1.0 / steps
    gram_ref[...] = (times(high[...], high[...]) + times(high[...], low[...]) + times(low[...], high[...])) * scale
    v_high = velocity.astype(jnp.bfloat16)
    v_low = (velocity - v_high.astype(jnp.float32)).astype(jnp.bfloat16)
    rhs_ref[...] = (times(v_high, high[...]) + times(v_high, low[...]) + times(v_low, high[...])) * scale


def shards(groups, blocks, snapshots, basis):
    rows_count, steps = snapshots.shape
    depth, modes = basis.shape
    owners = min(groups, modes // 2)
    share = modes // owners
    vmem = pltpu.CompilerParams(vmem_limit_bytes=40 << 20)
    projected = pl.pallas_call(
        functools.partial(project_kernel, groups, blocks, owners),
        out_shape=jax.ShapeDtypeStruct((modes, steps * blocks), jnp.float32),
        in_specs=[pl.BlockSpec(memory_space=pl.ANY)] * 2,
        out_specs=pl.BlockSpec(memory_space=pltpu.VMEM),
        scratch_shapes=[
            pltpu.VMEM((rows_count, steps), jnp.bfloat16),
            pltpu.VMEM((blocks, modes, depth), jnp.bfloat16),
            pltpu.VMEM((owners, share, steps), jnp.float32),
            pltpu.VMEM((groups - 1, share, steps), jnp.float32),
            pltpu.VMEM((blocks * owners, share, steps), jnp.float32),
            pltpu.SemaphoreType.DMA((blocks * CHUNKS,)),
            pltpu.SemaphoreType.DMA,
            pltpu.SemaphoreType.DMA((blocks - 1,)),
            pltpu.SemaphoreType.DMA((blocks - 1,)),
            pltpu.SemaphoreType.DMA,
            pltpu.SemaphoreType.DMA,
            pltpu.SemaphoreType.DMA,
            pltpu.SemaphoreType.DMA,
        ],
        compiler_params=pltpu.CompilerParams(collective_id=0, has_side_effects=True, vmem_limit_bytes=40 << 20),
    )(snapshots, basis.T)
    count = modes + modes * (modes + 1) // 2
    gram, rhs = pl.pallas_call(
        gram_kernel,
        out_shape=(jax.ShapeDtypeStruct((count, count), jnp.float32), jax.ShapeDtypeStruct((modes, count), jnp.float32)),
        in_specs=[pl.BlockSpec(memory_space=pltpu.VMEM)],
        out_specs=[pl.BlockSpec(memory_space=pltpu.VMEM)] * 2,
        scratch_shapes=[
            pltpu.VMEM((count, steps * blocks), jnp.float32),
            pltpu.VMEM((count, steps * blocks), jnp.bfloat16),
            pltpu.VMEM((count, steps * blocks), jnp.bfloat16),
        ],
        compiler_params=vmem,
    )(projected)
    return gram, rhs.T


def solution(mesh):
    step = functools.partial(shards, mesh.shape["rows"], mesh.shape["tm"])
    return jax.shard_map(step, mesh=mesh, in_specs=(P("rows", "tm"), P(("rows", "tm"), None)), out_specs=(P(), P()), check_vma=False)
```

time: 249 us -> 24.8 us (0.10)
  waiting for transfers between devices: 142 us -> 0 us
  blocking collectives: 77 us -> 0 us
  Pallas kernels: 0 us -> 20.7 us
  between operations: 14.1 us -> 0.65 us
  matrix products: 6.72 us -> 0 us
  other arithmetic: 4.73 us -> 0 us
    psum x1 -> x0, waiting for transfers between devices: 127 us -> none  [shards(): gram_sum, rhs_sum = lax.psum((gram_part, rhs_part), ('rows', 'tm'))]
    psum x1 -> x0, blocking collectives: 77 us -> none  [shards(): whole_proj, whole_vel = lax.psum((partial_value, velocity_part), 'rows')]
    pallas_call x0 -> x2, Pallas kernels: none -> 20.7 us  [the longest x1 18.5 us: shards(): pl.pallas_call(functools.partial(project_kernel, groups, blocks, owners),...]
    all_gather x1 -> x0, waiting for transfers between devices: 12 us -> none  [shards(): lax.all_gather(basis, 'tm', axis=0, tiled=True)]
    dot_general x3 -> x0, matrix products: 6.72 us -> none  [the longest x1 3.26 us: shards(): jnp.einsum('nr,nt->rt', lax.all_gather(basis, 'tm', axis=0, tiled=True),...]
    div x2 -> x0, other arithmetic: 3.22 us -> none  [shards(): return (gram_sum / total_steps, rhs_sum / total_steps)]
    unnamed x2 -> x4, local copies, waits for them, and re-layouts: 0.01 us -> 3.22 us
    gather x2 -> x0, local copies, waits for them, and re-layouts: 3.17 us -> none  [build_sums(): quadratic = series[:, upper_pair[0]] * series[:, upper_pair[1]]]
  transfers between devices with their start and end apart: 3 -> 0, of which waited for: 3 -> 0; matrix products, arithmetic and copies ran while one was open for 1% -> 0% of each run, Pallas kernels for 0% -> 0%
where the time goes in v1:
time: 24.8 us; the launch traced here: 24.6 us
  Pallas kernels  20.7 us (83%)
  local copies, waits for them, and re-layouts  3.22 us (13%)
  between operations  0.65 us (3%)
    pallas_call x1, Pallas kernels, shards(): pl.pallas_call(functools.partial(project_kernel, groups, blocks, owners),...  18.5 us
    unnamed x4, local copies, waits for them, and re-layouts  3.22 us
    pallas_call x1, Pallas kernels, shards(): pl.pallas_call(gram_kernel, out_shape=(jax.ShapeDtypeStruct((count, count...  2.26 us

profile of v1, /device:TPU:0, one launch (start us, length us, event | category | flops | bytes accessed | tf_op | source)
XLA Modules:
  0.0 24.6 jit_solution(10726136100811621876)
XLA Ops:
  0.6 0.0 copy-start
  0.6 2.2 %copy-done = bf16[16384,128]{1,0:T(8,128)(2,1)S(1)} copy-done((bf16[16384,128]{1,0:T(8,128)(2,1)S(1)}, bf16[16384,128]{1,0:T(8,128)(2,1)}, u32[]{:S(2)}) %copy-start) | copy-done | bytes 4194328
  2.8 0.0 copy-start.1
  2.8 1.0 %copy-done.1 = bf16[8192,32]{0,1:T(8,128)(2,1)S(1)} copy-done((bf16[8192,32]{0,1:T(8,128)(2,1)S(1)}, bf16[8192,32]{0,1:T(8,128)(2,1)}, u32[]{:S(2)}) %copy-start.1) | copy-done | bytes 524312
  3.9 18.5 %shard_map.41.proj_ref = f32[32,256]{1,0:T(8,128)S(1)} custom-call(bf16[16384,128]{1,0:T(8,128)(2,1)S(1)} %copy-done, bf16[32,8192]{1,0:T(8,128)(2,1)S(1)} %bitcast.2), custom_call_target="tpu_custom_call" | custom-call | tf_op jit(solution)/shard_map/pallas_call | solution.py:149
  22.3 2.3 %shard_map.42 = (f32[560,560]{1,0:T(8,128)}, f32[32,560]{1,0:T(8,128)}) custom-call(f32[32,256]{1,0:T(8,128)S(1)} %shard_map.41.proj_ref), custom_call_target="tpu_custom_call" | custom-call | tf_op jit(solution)/shard_map/pallas_call | solution.py:172
Async XLA Ops:
  0.6 2.2 %copy-start = (bf16[16384,128]{1,0:T(8,128)(2,1)S(1)}, bf16[16384,128]{1,0:T(8,128)(2,1)}, u32[]{:S(2)}) copy-start(bf16[16384,128]{1,0:T(8,128)(2,1)} %snap_hbm.1) | copy-start | bytes 12582916
  2.8 1.0 %copy-start.1 = (bf16[8192,32]{0,1:T(8,128)(2,1)S(1)}, bf16[8192,32]{0,1:T(8,128)(2,1)}, u32[]{:S(2)}) copy-start(bf16[8192,32]{0,1:T(8,128)(2,1)} %param.3) | copy-start | bytes 1572868

commit v2 on v1

v2 whole, which is shorter than its diff:
```python
import functools

import jax
import jax.numpy as jnp
from jax import lax
from jax.experimental import pallas as pl
from jax.experimental.pallas import tpu as pltpu
from jax.sharding import PartitionSpec as P

MESH = pl.DeviceIdType.MESH
CHUNKS = 4


def project_kernel(outer, inner, blocks, snap_hbm, basis_hbm, out_ref, snap, basis, part, landed, crossed, gathered,
                   snap_sem, basis_sem, send_basis, recv_basis, send_sem, recv_sem):
    row, block = lax.axis_index("rows"), lax.axis_index("tm")
    a, b = row // inner, lax.rem(row, inner)
    modes, depth = basis_hbm.shape
    share = modes // inner
    piece = depth // CHUNKS

    own_basis = pltpu.make_async_copy(basis_hbm, basis.at[block], basis_sem)
    own_basis.start()
    loads = []
    for i in range(blocks):
        at = lax.rem(block + i, blocks)
        for c in range(CHUNKS):
            span = pl.ds(pl.multiple_of(at * depth + c * piece, 256), piece)
            load = pltpu.make_async_copy(snap_hbm.at[span], snap.at[span], snap_sem.at[i * CHUNKS + c])
            load.start()
            loads.append((load, span))

    across = [(lax.rem(a + d, outer) * inner + b, block) for d in range(1, outer)]
    within = []
    for e in range(blocks):
        for d in range(inner):
            if d or e:
                within.append((a * inner + lax.rem(b + d, inner), lax.rem(block + e, blocks)))
    barrier = pltpu.get_barrier_semaphore()
    for device in within + across:
        pl.semaphore_signal(barrier, inc=1, device_id=device, device_id_type=MESH)
    own_basis.wait()
    pl.semaphore_wait(barrier, len(within) + len(across))

    sends = []
    for d in range(1, blocks):
        send = pltpu.make_async_remote_copy(
            src_ref=basis.at[block], dst_ref=basis.at[block], send_sem=send_basis.at[d - 1], recv_sem=recv_basis.at[d - 1],
            device_id=(row, lax.rem(block + d, blocks)), device_id_type=MESH)
        send.start()
        sends.append(send)

    total = jnp.zeros((modes, snap.shape[1]), jnp.float32)
    for i in range(blocks):
        at = lax.rem(block + i, blocks)
        if i > 0:
            pltpu.make_async_copy(basis.at[at], basis.at[at], recv_basis.at[blocks - i - 1]).wait()
        for c in range(CHUNKS):
            load, span = loads[i * CHUNKS + c]
            load.wait()
            total += jnp.dot(basis[at, :, c * piece:(c + 1) * piece], snap[span, :], preferred_element_type=jnp.float32)
    for k in range(inner):
        part[k] = total[k * share:(k + 1) * share]

    def send_to(stage, source, target, device):
        pltpu.make_async_remote_copy(
            src_ref=source, dst_ref=target, send_sem=send_sem.at[stage], recv_sem=recv_sem.at[stage],
            device_id=device, device_id_type=MESH).start()

    def wait_all(ref, semaphore):
        pltpu.make_async_copy(ref, ref, semaphore).wait()

    for d in range(1, inner):
        owner = lax.rem(b + d, inner)
        send_to(0, part.at[owner], landed.at[inner - d - 1], (a * inner + owner, block))
    wait_all(landed, recv_sem.at[0])
    crossed[a] = part[b] + jnp.sum(landed[...], axis=0)

    for device in across:
        send_to(1, crossed.at[a], crossed.at[a], device)
    wait_all(crossed.at[pl.ds(0, outer - 1)], recv_sem.at[1])
    mine = block * inner + b
    gathered[mine] = jnp.sum(crossed[...], axis=0)

    for device in within:
        send_to(2, gathered.at[mine], gathered.at[mine], device)
    rest = gathered.at[pl.ds(0, inner * blocks - 1)]
    wait_all(rest, recv_sem.at[2])
    steps = snap.shape[1]
    for t in range(blocks):
        for k in range(inner):
            out_ref[k * share:(k + 1) * share, t * steps:(t + 1) * steps] = gathered[t * inner + k]

    for send in sends:
        send.wait_send()
    wait_all(landed, send_sem.at[0])
    wait_all(crossed.at[pl.ds(0, outer - 1)], send_sem.at[1])
    wait_all(rest, send_sem.at[2])


def gram_kernel(proj_ref, gram_ref, rhs_ref, features, high, low):
    modes, steps = proj_ref.shape
    projected = proj_ref[...]
    velocity = pltpu.roll(projected, steps - 1, 1) - projected
    series = jnp.where(lax.broadcasted_iota(jnp.int32, projected.shape, 1) < steps - 1, projected, 0.0)
    features[0:modes, :] = series
    at = modes
    for i in range(modes):
        features[at:at + modes - i, :] = series[i:i + 1, :] * series[i:, :]
        at += modes - i
    whole = features[...]
    top = whole.astype(jnp.bfloat16)
    high[...] = top
    low[...] = (whole - top.astype(jnp.float32)).astype(jnp.bfloat16)

    def times(a, b):
        return lax.dot_general(a, b, (((1,), (1,)), ((), ())), preferred_element_type=jnp.float32)

    scale = 1.0 / steps
    gram_ref[...] = (times(high[...], high[...]) + times(high[...], low[...]) + times(low[...], high[...])) * scale
    v_high = velocity.astype(jnp.bfloat16)
    v_low = (velocity - v_high.astype(jnp.float32)).astype(jnp.bfloat16)
    rhs_ref[...] = (times(v_high, high[...]) + times(v_high, low[...]) + times(v_low, high[...])) * scale


def shards(groups, blocks, snapshots, basis):
    rows_count, steps = snapshots.shape
    depth, modes = basis.shape
    inner = 1
    while inner * inner < groups:
        inner *= 2
    outer = groups // inner
    share = modes // inner
    vmem = pltpu.CompilerParams(vmem_limit_bytes=40 << 20)
    projected = pl.pallas_call(
        functools.partial(project_kernel, outer, inner, blocks),
        out_shape=jax.ShapeDtypeStruct((modes, steps * blocks), jnp.float32),
        in_specs=[pl.BlockSpec(memory_space=pltpu.HBM)] * 2,
        out_specs=pl.BlockSpec(memory_space=pltpu.VMEM),
        scratch_shapes=[
            pltpu.VMEM((rows_count, steps), jnp.bfloat16),
            pltpu.VMEM((blocks, modes, depth), jnp.bfloat16),
            pltpu.VMEM((inner, share, steps), jnp.float32),
            pltpu.VMEM((inner - 1, share, steps), jnp.float32),
            pltpu.VMEM((outer, share, steps), jnp.float32),
            pltpu.VMEM((blocks * inner, share, steps), jnp.float32),
            pltpu.SemaphoreType.DMA((blocks * CHUNKS,)),
            pltpu.SemaphoreType.DMA,
            pltpu.SemaphoreType.DMA((blocks - 1,)),
            pltpu.SemaphoreType.DMA((blocks - 1,)),
            pltpu.SemaphoreType.DMA((3,)),
            pltpu.SemaphoreType.DMA((3,)),
        ],
        compiler_params=pltpu.CompilerParams(collective_id=0, has_side_effects=True, vmem_limit_bytes=40 << 20),
    )(snapshots, basis.T)
    count = modes + modes * (modes + 1) // 2
    gram, rhs = pl.pallas_call(
        gram_kernel,
        out_shape=(jax.ShapeDtypeStruct((count, count), jnp.float32), jax.ShapeDtypeStruct((modes, count), jnp.float32)),
        in_specs=[pl.BlockSpec(memory_space=pltpu.VMEM)],
        out_specs=[pl.BlockSpec(memory_space=pltpu.VMEM)] * 2,
        scratch_shapes=[
            pltpu.VMEM((count, steps * blocks), jnp.float32),
            pltpu.VMEM((count, steps * blocks), jnp.bfloat16),
            pltpu.VMEM((count, steps * blocks), jnp.bfloat16),
        ],
        compiler_params=vmem,
    )(projected)
    return gram, rhs.T


def solution(mesh):
    step = functools.partial(shards, mesh.shape["rows"], mesh.shape["tm"])
    return jax.shard_map(step, mesh=mesh, in_specs=(P("rows", "tm"), P(("rows", "tm"), None)), out_specs=(P(), P()), check_vma=False)
```

time: 24.8 us -> 24.5 us (0.988)
  Pallas kernels: 20.7 us -> 20.4 us
    pallas_call x1, Pallas kernels: 18.5 us -> 18.1 us  [shards(): pl.pallas_call(functools.partial(project_kernel, outer, inner, blocks), o...]
where the time goes in v2:
time: 24.5 us; the launch traced here: 24.3 us
  Pallas kernels  20.4 us (83%)
  local copies, waits for them, and re-layouts  3.22 us (13%)
  between operations  0.65 us (3%)
    pallas_call x1, Pallas kernels, shards(): pl.pallas_call(functools.partial(project_kernel, outer, inner, blocks), o...  18.1 us
    unnamed x4, local copies, waits for them, and re-layouts  3.22 us
    pallas_call x1, Pallas kernels, shards(): pl.pallas_call(gram_kernel, out_shape=(jax.ShapeDtypeStruct((count, count...  2.27 us

profile of v2, /device:TPU:0, one launch (start us, length us, event | category | flops | bytes accessed | tf_op | source)
XLA Modules:
  0.0 24.3 jit_solution(4833484074194648617)
XLA Ops:
  0.6 0.0 copy-start
  0.6 2.2 %copy-done = bf16[16384,128]{1,0:T(8,128)(2,1)S(1)} copy-done((bf16[16384,128]{1,0:T(8,128)(2,1)S(1)}, bf16[16384,128]{1,0:T(8,128)(2,1)}, u32[]{:S(2)}) %copy-start) | copy-done | bytes 4194328
  2.8 0.0 copy-start.1
  2.8 1.0 %copy-done.1 = bf16[8192,32]{0,1:T(8,128)(2,1)S(1)} copy-done((bf16[8192,32]{0,1:T(8,128)(2,1)S(1)}, bf16[8192,32]{0,1:T(8,128)(2,1)}, u32[]{:S(2)}) %copy-start.1) | copy-done | bytes 524312
  3.9 18.1 %shard_map.41.proj_ref = f32[32,256]{1,0:T(8,128)S(1)} custom-call(bf16[16384,128]{1,0:T(8,128)(2,1)S(1)} %copy-done, bf16[32,8192]{1,0:T(8,128)(2,1)S(1)} %bitcast.2), custom_call_target="tpu_custom_call" | custom-call | tf_op jit(solution)/shard_map/pallas_call | solution.py:135
  22.0 2.3 %shard_map.42 = (f32[560,560]{1,0:T(8,128)}, f32[32,560]{1,0:T(8,128)}) custom-call(f32[32,256]{1,0:T(8,128)S(1)} %shard_map.41.proj_ref), custom_call_target="tpu_custom_call" | custom-call | tf_op jit(solution)/shard_map/pallas_call | solution.py:157
Async XLA Ops:
  0.6 2.2 %copy-start = (bf16[16384,128]{1,0:T(8,128)(2,1)S(1)}, bf16[16384,128]{1,0:T(8,128)(2,1)}, u32[]{:S(2)}) copy-start(bf16[16384,128]{1,0:T(8,128)(2,1)} %snap_hbm.1) | copy-start | bytes 12582916
  2.8 1.0 %copy-start.1 = (bf16[8192,32]{0,1:T(8,128)(2,1)S(1)}, bf16[8192,32]{0,1:T(8,128)(2,1)}, u32[]{:S(2)}) copy-start(bf16[8192,32]{0,1:T(8,128)(2,1)} %param.3) | copy-start | bytes 1572868

commit v3 on v2

--- a/solution.py
+++ b/solution.py
@@ -152,7 +152,7 @@
             pltpu.SemaphoreType.DMA((3,)),
         ],
         compiler_params=pltpu.CompilerParams(collective_id=0, has_side_effects=True, vmem_limit_bytes=40 << 20),
-    )(snapshots, basis.T)
+    )(pltpu.with_memory_space_constraint(snapshots, pltpu.HBM), pltpu.with_memory_space_constraint(basis.T, pltpu.HBM))
     count = modes + modes * (modes + 1) // 2
     gram, rhs = pl.pallas_call(
         gram_kernel,

time: 24.5 us -> 20.9 us (0.85)
  local copies, waits for them, and re-layouts: 3.22 us -> 0 us
  Pallas kernels: 20.4 us -> 20.1 us
    unnamed x4 -> x0, local copies, waits for them, and re-layouts: 3.22 us -> none
    pallas_call x1, Pallas kernels: 18.1 us -> 17.8 us  [shards(): pl.pallas_call(functools.partial(project_kernel, outer, inner, blocks), o...]
where the time goes in v3:
time: 20.9 us; the launch traced here: 20.7 us
  Pallas kernels  20.1 us (96%)
  between operations  0.64 us (3%)
    pallas_call x1, Pallas kernels, shards(): pl.pallas_call(functools.partial(project_kernel, outer, inner, blocks), o...  17.8 us
    pallas_call x1, Pallas kernels, shards(): pl.pallas_call(gram_kernel, out_shape=(jax.ShapeDtypeStruct((count, count...  2.27 us

profile of v3, /device:TPU:0, one launch (start us, length us, event | category | flops | bytes accessed | tf_op | source)
XLA Modules:
  0.0 20.7 jit_solution(1056685365774566648)
XLA Ops:
  0.6 17.8 %shard_map.41.proj_ref = f32[32,256]{1,0:T(8,128)S(1)} custom-call(bf16[16384,128]{1,0:T(8,128)(2,1)} %snap_hbm.1, bf16[32,8192]{1,0:T(8,128)(2,1)} %bitcast.2), custom_call_target="tpu_custom_call" | custom-call | tf_op jit(solution)/shard_map/pallas_call | solution.py:135
  18.5 2.3 %shard_map.42 = (f32[560,560]{1,0:T(8,128)}, f32[32,560]{1,0:T(8,128)}) custom-call(f32[32,256]{1,0:T(8,128)S(1)} %shard_map.41.proj_ref), custom_call_target="tpu_custom_call" | custom-call | tf_op jit(solution)/shard_map/pallas_call | solution.py:157

commit v4 on v3

--- a/solution.py
+++ b/solution.py
@@ -11,12 +11,11 @@
 CHUNKS = 4
 
 
-def project_kernel(outer, inner, blocks, snap_hbm, basis_hbm, out_ref, snap, basis, part, landed, crossed, gathered,
+def project_kernel(outer, inner, blocks, snap_hbm, basis_hbm, out_ref, snap, basis, crossed, gathered,
                    snap_sem, basis_sem, send_basis, recv_basis, send_sem, recv_sem):
     row, block = lax.axis_index("rows"), lax.axis_index("tm")
     a, b = row // inner, lax.rem(row, inner)
     modes, depth = basis_hbm.shape
-    share = modes // inner
     piece = depth // CHUNKS
 
     own_basis = pltpu.make_async_copy(basis_hbm, basis.at[block], basis_sem)
@@ -59,8 +58,7 @@
             load, span = loads[i * CHUNKS + c]
             load.wait()
             total += jnp.dot(basis[at, :, c * piece:(c + 1) * piece], snap[span, :], preferred_element_type=jnp.float32)
-    for k in range(inner):
-        part[k] = total[k * share:(k + 1) * share]
+    crossed[a] = total
 
     def send_to(stage, source, target, device):
         pltpu.make_async_remote_copy(
@@ -70,32 +68,24 @@
     def wait_all(ref, semaphore):
         pltpu.make_async_copy(ref, ref, semaphore).wait()
 
-    for d in range(1, inner):
-        owner = lax.rem(b + d, inner)
-        send_to(0, part.at[owner], landed.at[inner - d - 1], (a * inner + owner, block))
-    wait_all(landed, recv_sem.at[0])
-    crossed[a] = part[b] + jnp.sum(landed[...], axis=0)
-
     for device in across:
-        send_to(1, crossed.at[a], crossed.at[a], device)
-    wait_all(crossed.at[pl.ds(0, outer - 1)], recv_sem.at[1])
+        send_to(0, crossed.at[a], crossed.at[a], device)
+    wait_all(crossed.at[pl.ds(0, outer - 1)], recv_sem.at[0])
     mine = block * inner + b
     gathered[mine] = jnp.sum(crossed[...], axis=0)
 
     for device in within:
-        send_to(2, gathered.at[mine], gathered.at[mine], device)
+        send_to(1, gathered.at[mine], gathered.at[mine], device)
     rest = gathered.at[pl.ds(0, inner * blocks - 1)]
-    wait_all(rest, recv_sem.at[2])
+    wait_all(rest, recv_sem.at[1])
     steps = snap.shape[1]
     for t in range(blocks):
-        for k in range(inner):
-            out_ref[k * share:(k + 1) * share, t * steps:(t + 1) * steps] = gathered[t * inner + k]
+        out_ref[:, t * steps:(t + 1) * steps] = jnp.sum(gathered[t * inner:(t + 1) * inner], axis=0)
 
     for send in sends:
         send.wait_send()
-    wait_all(landed, send_sem.at[0])
-    wait_all(crossed.at[pl.ds(0, outer - 1)], send_sem.at[1])
-    wait_all(rest, send_sem.at[2])
+    wait_all(crossed.at[pl.ds(0, outer - 1)], send_sem.at[0])
+    wait_all(rest, send_sem.at[1])
 
 
 def gram_kernel(proj_ref, gram_ref, rhs_ref, features, high, low):
@@ -130,7 +120,6 @@
     while inner * inner < groups:
         inner *= 2
     outer = groups // inner
-    share = modes // inner
     vmem = pltpu.CompilerParams(vmem_limit_bytes=40 << 20)
     projected = pl.pallas_call(
         functools.partial(project_kernel, outer, inner, blocks),
@@ -140,16 +129,14 @@
         scratch_shapes=[
             pltpu.VMEM((rows_count, steps), jnp.bfloat16),
             pltpu.VMEM((blocks, modes, depth), jnp.bfloat16),
-            pltpu.VMEM((inner, share, steps), jnp.float32),
-            pltpu.VMEM((inner - 1, share, steps), jnp.float32),
-            pltpu.VMEM((outer, share, steps), jnp.float32),
-            pltpu.VMEM((blocks * inner, share, steps), jnp.float32),
+            pltpu.VMEM((outer, modes, steps), jnp.float32),
+            pltpu.VMEM((blocks * inner, modes, steps), jnp.float32),
             pltpu.SemaphoreType.DMA((blocks * CHUNKS,)),
             pltpu.SemaphoreType.DMA,
             pltpu.SemaphoreType.DMA((blocks - 1,)),
             pltpu.SemaphoreType.DMA((blocks - 1,)),
-            pltpu.SemaphoreType.DMA((3,)),
-            pltpu.SemaphoreType.DMA((3,)),
+            pltpu.SemaphoreType.DMA((2,)),
+            pltpu.SemaphoreType.DMA((2,)),
         ],
         compiler_params=pltpu.CompilerParams(collective_id=0, has_side_effects=True, vmem_limit_bytes=40 << 20),
     )(pltpu.with_memory_space_constraint(snapshots, pltpu.HBM), pltpu.with_memory_space_constraint(basis.T, pltpu.HBM))

time: 20.9 us -> 18.2 us (0.87)
  Pallas kernels: 20.1 us -> 17.4 us
    pallas_call x1, Pallas kernels: 17.8 us -> 15.1 us  [shards(): pl.pallas_call(functools.partial(project_kernel, outer, inner, blocks), o...]
where the time goes in v4:
time: 18.2 us; the launch traced here: 18 us
  Pallas kernels  17.4 us (96%)
  between operations  0.64 us (4%)
    pallas_call x1, Pallas kernels, shards(): pl.pallas_call(functools.partial(project_kernel, outer, inner, blocks), o...  15.1 us
    pallas_call x1, Pallas kernels, shards(): pl.pallas_call(gram_kernel, out_shape=(jax.ShapeDtypeStruct((count, count...  2.27 us

profile of v4, /device:TPU:0, one launch (start us, length us, event | category | flops | bytes accessed | tf_op | source)
XLA Modules:
  0.0 18.0 jit_solution(11422380250230946633)
XLA Ops:
  0.6 15.1 %shard_map.41.proj_ref = f32[32,256]{1,0:T(8,128)S(1)} custom-call(bf16[16384,128]{1,0:T(8,128)(2,1)} %snap_hbm.1, bf16[32,8192]{1,0:T(8,128)(2,1)} %bitcast.2), custom_call_target="tpu_custom_call" | custom-call | tf_op jit(solution)/shard_map/pallas_call | solution.py:124
  15.8 2.3 %shard_map.42 = (f32[560,560]{1,0:T(8,128)}, f32[32,560]{1,0:T(8,128)}) custom-call(f32[32,256]{1,0:T(8,128)S(1)} %shard_map.41.proj_ref), custom_call_target="tpu_custom_call" | custom-call | tf_op jit(solution)/shard_map/pallas_call | solution.py:144

commit v5 on v4

--- a/solution.py
+++ b/solution.py
@@ -8,7 +8,7 @@
 from jax.sharding import PartitionSpec as P
 
 MESH = pl.DeviceIdType.MESH
-CHUNKS = 4
+CHUNKS = 2
 
 
 def project_kernel(outer, inner, blocks, snap_hbm, basis_hbm, out_ref, snap, basis, crossed, gathered,

time: 18.2 us -> 17.9 us (0.984)
  Pallas kernels: 17.4 us -> 17.1 us
    pallas_call x1, Pallas kernels: 15.1 us -> 14.8 us  [shards(): pl.pallas_call(functools.partial(project_kernel, outer, inner, blocks), o...]
where the time goes in v5:
time: 17.9 us; the launch traced here: 17.7 us
  Pallas kernels  17.1 us (96%)
  between operations  0.64 us (4%)
    pallas_call x1, Pallas kernels, shards(): pl.pallas_call(functools.partial(project_kernel, outer, inner, blocks), o...  14.8 us
    pallas_call x1, Pallas kernels, shards(): pl.pallas_call(gram_kernel, out_shape=(jax.ShapeDtypeStruct((count, count...  2.27 us

profile of v5, /device:TPU:0, one launch (start us, length us, event | category | flops | bytes accessed | tf_op | source)
XLA Modules:
  0.0 17.7 jit_solution(10933123590080150399)
XLA Ops:
  0.6 14.8 %shard_map.41.proj_ref = f32[32,256]{1,0:T(8,128)S(1)} custom-call(bf16[16384,128]{1,0:T(8,128)(2,1)} %snap_hbm.1, bf16[32,8192]{1,0:T(8,128)(2,1)} %bitcast.2), custom_call_target="tpu_custom_call" | custom-call | tf_op jit(solution)/shard_map/pallas_call | solution.py:124
  15.4 2.3 %shard_map.42 = (f32[560,560]{1,0:T(8,128)}, f32[32,560]{1,0:T(8,128)}) custom-call(f32[32,256]{1,0:T(8,128)S(1)} %shard_map.41.proj_ref), custom_call_target="tpu_custom_call" | custom-call | tf_op jit(solution)/shard_map/pallas_call | solution.py:144

commit v6 on v5

--- a/solution.py
+++ b/solution.py
@@ -88,7 +88,7 @@
     wait_all(rest, send_sem.at[1])
 
 
-def gram_kernel(proj_ref, gram_ref, rhs_ref, features, high, low):
+def gram_kernel(proj_ref, gram_ref, rhs_ref, features, left, right):
     modes, steps = proj_ref.shape
     projected = proj_ref[...]
     velocity = pltpu.roll(projected, steps - 1, 1) - projected
@@ -98,19 +98,19 @@
     for i in range(modes):
         features[at:at + modes - i, :] = series[i:i + 1, :] * series[i:, :]
         at += modes - i
+    features[at:at + modes, :] = velocity
     whole = features[...]
-    top = whole.astype(jnp.bfloat16)
-    high[...] = top
-    low[...] = (whole - top.astype(jnp.float32)).astype(jnp.bfloat16)
-
-    def times(a, b):
-        return lax.dot_general(a, b, (((1,), (1,)), ((), ())), preferred_element_type=jnp.float32)
-
-    scale = 1.0 / steps
-    gram_ref[...] = (times(high[...], high[...]) + times(high[...], low[...]) + times(low[...], high[...])) * scale
-    v_high = velocity.astype(jnp.bfloat16)
-    v_low = (velocity - v_high.astype(jnp.float32)).astype(jnp.bfloat16)
-    rhs_ref[...] = (times(v_high, high[...]) + times(v_high, low[...]) + times(v_low, high[...])) * scale
+    high = whole.astype(jnp.bfloat16)
+    low = (whole - high.astype(jnp.float32)).astype(jnp.bfloat16)
+    left[:, 0:steps] = high
+    left[:, steps:2 * steps] = high
+    left[:, 2 * steps:3 * steps] = low
+    right[:, 0:steps] = high[0:at]
+    right[:, steps:2 * steps] = low[0:at]
+    right[:, 2 * steps:3 * steps] = high[0:at]
+    sums = lax.dot_general(left[...], right[...], (((1,), (1,)), ((), ())), preferred_element_type=jnp.float32) * (1.0 / steps)
+    gram_ref[...] = sums[0:at]
+    rhs_ref[...] = sums[at:]
 
 
 def shards(groups, blocks, snapshots, basis):
@@ -147,9 +147,9 @@
         in_specs=[pl.BlockSpec(memory_space=pltpu.VMEM)],
         out_specs=[pl.BlockSpec(memory_space=pltpu.VMEM)] * 2,
         scratch_shapes=[
-            pltpu.VMEM((count, steps * blocks), jnp.float32),
-            pltpu.VMEM((count, steps * blocks), jnp.bfloat16),
-            pltpu.VMEM((count, steps * blocks), jnp.bfloat16),
+            pltpu.VMEM((count + modes, steps * blocks), jnp.float32),
+            pltpu.VMEM((count + modes, 3 * steps * blocks), jnp.bfloat16),
+            pltpu.VMEM((count, 3 * steps * blocks), jnp.bfloat16),
         ],
         compiler_params=vmem,
     )(projected)

time: 17.9 us -> 17.6 us (0.983)
  Pallas kernels: 17.1 us -> 16.8 us
    pallas_call x1, Pallas kernels: 2.27 us -> 2.03 us  [shards(): pl.pallas_call(gram_kernel, out_shape=(jax.ShapeDtypeStruct((count, count...]
where the time goes in v6:
time: 17.6 us; the launch traced here: 17.5 us
  Pallas kernels  16.8 us (95%)
  between operations  0.64 us (4%)
    pallas_call x1, Pallas kernels, shards(): pl.pallas_call(functools.partial(project_kernel, outer, inner, blocks), o...  14.8 us
    pallas_call x1, Pallas kernels, shards(): pl.pallas_call(gram_kernel, out_shape=(jax.ShapeDtypeStruct((count, count...  2.03 us

profile of v6, /device:TPU:0, one launch (start us, length us, event | category | flops | bytes accessed | tf_op | source)
XLA Modules:
  0.0 17.5 jit_solution(4135871821762571127)
XLA Ops:
  0.6 14.8 %shard_map.41.proj_ref = f32[32,256]{1,0:T(8,128)S(1)} custom-call(bf16[16384,128]{1,0:T(8,128)(2,1)} %snap_hbm.1, bf16[32,8192]{1,0:T(8,128)(2,1)} %bitcast.2), custom_call_target="tpu_custom_call" | custom-call | tf_op jit(solution)/shard_map/pallas_call | solution.py:124
  15.4 2.0 %shard_map.42 = (f32[560,560]{1,0:T(8,128)}, f32[32,560]{1,0:T(8,128)}) custom-call(f32[32,256]{1,0:T(8,128)S(1)} %shard_map.41.proj_ref), custom_call_target="tpu_custom_call" | custom-call | tf_op jit(solution)/shard_map/pallas_call | solution.py:144

commit v7 on v6

--- a/solution.py
+++ b/solution.py
@@ -31,8 +31,8 @@
 
     across = [(lax.rem(a + d, outer) * inner + b, block) for d in range(1, outer)]
     within = []
-    for e in range(blocks):
-        for d in range(inner):
+    for d in range(inner - 1, -1, -1):
+        for e in range(blocks):
             if d or e:
                 within.append((a * inner + lax.rem(b + d, inner), lax.rem(block + e, blocks)))
     barrier = pltpu.get_barrier_semaphore()

time: 17.6 us -> 18 us (1.023)
  Pallas kernels: 16.8 us -> 17.2 us
    pallas_call x1, Pallas kernels: 14.8 us -> 15.1 us  [shards(): pl.pallas_call(functools.partial(project_kernel, outer, inner, blocks), o...]
where the time goes in v7:
time: 18 us; the launch traced here: 17.8 us
  Pallas kernels  17.2 us (96%)
  between operations  0.64 us (4%)
    pallas_call x1, Pallas kernels, shards(): pl.pallas_call(functools.partial(project_kernel, outer, inner, blocks), o...  15.1 us
    pallas_call x1, Pallas kernels, shards(): pl.pallas_call(gram_kernel, out_shape=(jax.ShapeDtypeStruct((count, count...  2.03 us

profile of v7, /device:TPU:0, one launch (start us, length us, event | category | flops | bytes accessed | tf_op | source)
XLA Modules:
  0.0 17.8 jit_solution(17939724817114321474)
XLA Ops:
  0.6 15.1 %shard_map.41.proj_ref = f32[32,256]{1,0:T(8,128)S(1)} custom-call(bf16[16384,128]{1,0:T(8,128)(2,1)} %snap_hbm.1, bf16[32,8192]{1,0:T(8,128)(2,1)} %bitcast.2), custom_call_target="tpu_custom_call" | custom-call | tf_op jit(solution)/shard_map/pallas_call | solution.py:124
  15.8 2.0 %shard_map.42 = (f32[560,560]{1,0:T(8,128)}, f32[32,560]{1,0:T(8,128)}) custom-call(f32[32,256]{1,0:T(8,128)S(1)} %shard_map.41.proj_ref), custom_call_target="tpu_custom_call" | custom-call | tf_op jit(solution)/shard_map/pallas_call | solution.py:144
